TPU v7x, 512 devices: a whole 4x4x16 slice. The times are simulated.
512 devices in a mesh: chan: 32 (over z_lo, x), tm: 16 (over z_hi, y, core).
Axes of the slice: x: 4, y: 4, z: 16 (z_hi: 2, z_lo: 8; z = z_hi * 8 + z_lo), core: 2. Of those that a mesh axis runs over, the one named last changes fastest.
Arguments:
- samples: bfloat16 [8192, 65536], P('chan', 'tm'), as said below
Outputs:
- coherence: float32 [16, 4, 2, 8192, 256], P('tm', None, None, 'chan')
Inputs may be any that keep to these rules, and one draw needn't show every extreme that they name: Real-valued samples of the fibre's channels.
All inputs are finite; a program needn't handle non-finite values.
Results may differ from a plain program's by a relative error of at most 0.00095.
Values may be sent and summed in bfloat16 or wider, within the bound.
A program may use at most 64 MiB of HBM per device.

v0:
```python
import math

import jax
import jax.numpy as jnp
from jax import lax
from jax.sharding import PartitionSpec as P

NFFT = 256
TAPS = 16
ROUNDS = 3
BINS = 128


epsilon = 1e-06


def shifted(block, axis, distance):
    devices = range(lax.axis_size(axis))
    route = [(i - distance, i) for i in devices if i - distance in devices]
    return lax.ppermute(block, axis, route)


def from_behind(value, axis, steps):
    count = lax.axis_size(axis)
    pairs = [(source, (source + steps) % count) for source in range(count)]
    return lax.ppermute(value, axis, pairs)


def prototype():
    length = TAPS * NFFT
    sample_index = jnp.arange(length, dtype=jnp.float32)
    centred = (sample_index + 0.5 - 0.5 * length) / NFFT
    window = jnp.sinc(centred) * (0.5 + 0.5 * jnp.cos(2.0 * math.pi * centred / TAPS))
    return window.reshape(TAPS, NFFT)


def transform_table():
    frequency = jnp.arange(BINS, dtype=jnp.int32)[:, None]
    position = jnp.arange(NFFT, dtype=jnp.int32)[None, :]
    phases = (frequency * position % NFFT).astype(jnp.float32) * (2.0 * math.pi / NFFT)
    return jnp.concatenate([jnp.cos(phases), -jnp.sin(phases)], 0).astype(jnp.bfloat16)


def filter_frames(extended, taps_table, sub_count):
    summed = jnp.zeros((extended.shape[0], sub_count, extended.shape[2]), jnp.float32)
    for offset in range(TAPS):
        summed = summed + taps_table[offset] * extended[:, offset : offset + sub_count, :].astype(
            jnp.float32
        )
    return summed.astype(jnp.bfloat16)


def on_device(samples):
    taps_table = prototype()
    fourier = transform_table()
    channels = samples.shape[0]
    sub_count = samples.shape[1] // NFFT
    local_blocks = samples.reshape(channels, sub_count, NFFT)
    earlier = shifted(local_blocks[:, sub_count - (TAPS - 1) :, :], "tm", 1)
    extended = jnp.concatenate([earlier, local_blocks], 1)
    frames = filter_frames(extended, taps_table, sub_count)
    spectra = jnp.einsum("fn,csn->fsc", fourier, frames, preferred_element_type=jnp.float32).astype(
        jnp.bfloat16
    )
    spectra = spectra.reshape(2, BINS, sub_count, channels)
    banded = lax.all_to_all(spectra, "tm", split_axis=1, concat_axis=2, tiled=True)
    values = banded.astype(jnp.float32)
    power_mean = jnp.mean(values[0] * values[0] + values[1] * values[1], axis=1)
    whitened = (values * lax.rsqrt(power_mean + epsilon)[None, :, None, :]).astype(jnp.bfloat16)
    inverse_count = 1.0 / banded.shape[2]
    own_rows = whitened.reshape(-1, channels)
    turned = jnp.concatenate([whitened[1], -whitened[0]], 0).reshape(-1, channels)
    dimensions = (((0,), (0,)), ((), ()))

    def coherence(partner):
        stacked = partner.reshape(-1, channels)
        real_part = lax.dot_general(
            own_rows, stacked, dimensions, preferred_element_type=jnp.float32
        )
        imag_part = lax.dot_general(turned, stacked, dimensions, preferred_element_type=jnp.float32)
        return jnp.stack([real_part, imag_part]) * inverse_count

    results = [coherence(whitened)]
    for distance in range(1, ROUNDS + 1):
        partner = from_behind(whitened, "chan", distance)
        results.append(coherence(partner))
    return jnp.stack(results)[None]


def solution(mesh):
    return jax.shard_map(
        on_device,
        mesh=mesh,
        in_specs=(P("chan", "tm"),),
        out_specs=P("tm", None, None, "chan", None),
        check_vma=False,
    )
```

profile of v0, /device:TPU:64, one launch (start us, length us, event | category | flops | bytes accessed | tf_op | source)
XLA Modules:
  0.0 481.7 jit_solution(18131543381212208522)
XLA Ops:
  0.0 1.8 copy.47
  2.0 2.0 collective-permute-start
  4.1 0.5 negate_convert_fusion
  4.7 2.8 collective-permute-done
  7.8 7.8 %fusion.8 = bf16[256,16,256]{0,2,1:T(8,128)(2,1)S(1)} fusion(bf16[256,31,256]{2,0,1:T(8,128)(2,1)S(1)} %constant_dynamic-update-slice_fusion, f32[256]{0:T(256)S(1)} %get-tuple-element.8, f32[256]{0:T(256)S(1)} %get-tuple-element.9, f32[256]{0:T(256)S(1)} %get-tuple-element.10, f32[256]{0:T(256)S(1)} %get-tuple-element.11, f32[256]{0:T(256)S(1)} %get-tuple-element.12, ...), kind=kOutput, calls=%fused_computation.17 | convolution fusion | flops 588513280 | bytes 35799040 | tf_op jit(solution)/shard_map/fn,csn->fsc/dot_general | solution.py:62
  15.6 1.2 copy.21
  16.8 104.9 %all_to_all.4 = bf16[2,128,16,256]{3,2,0,1:T(8,128)(2,1)S(1)} all-to-all(bf16[2,128,16,256]{3,2,0,1:T(8,128)(2,1)S(1)} %copy.21), channel_id=1, replica_groups=mesh['chan'=32,'tm'=16] {'tm'}, dimensions={1} | all-to-all | bytes 4194304 | tf_op jit(solution)/shard_map/all_to_all | solution.py:66
  121.9 0.6 convert_bitcast_fusion
  123.0 0.6 copy.25
  123.7 0.7 fusion.1
  124.4 4.7 collective-permute-start.3
  129.1 111.7 %collective-permute-start.2 = (bf16[2,8,256,256]{3,2,1,0:T(8,128)(2,1)S(1)}, bf16[2,8,256,256]{3,2,1,0:T(8,128)(2,1)S(1)}, u32[]{:S(2)}, u32[]{:S(2)}) collective-permute-start(bf16[2,8,256,256]{3,2,1,0:T(8,128)(2,1)S(1)} %fusion.1), channel_id=1, source_target_pairs={{0,32},{16,48},{32,64},{48,80},{64,96},{80,112},{96,128},{112,144}... | collective-permute-start | bytes 6291464 | tf_op jit(solution)/shard_map/ppermute | solution.py:26
  241.0 47.9 %collective-permute-start.1 = (bf16[2,8,256,256]{3,2,1,0:T(8,128)(2,1)S(1)}, bf16[2,8,256,256]{3,2,1,0:T(8,128)(2,1)S(1)}, u32[]{:S(2)}, u32[]{:S(2)}) collective-permute-start(bf16[2,8,256,256]{3,2,1,0:T(8,128)(2,1)S(1)} %fusion.1), channel_id=1, source_target_pairs={{0,16},{16,32},{32,48},{48,64},{64,80},{80,96},{96,112},{112,128},... | collective-permute-start | bytes 6291464 | tf_op jit(solution)/shard_map/ppermute | solution.py:26
  289.1 0.7 convolution_bitcast_fusion.6
  289.8 0.9 fusion.9
  290.8 15.3 %collective-permute-done.3 = bf16[2,8,256,256]{3,2,1,0:T(8,128)(2,1)S(1)} collective-permute-done((bf16[2,8,256,256]{3,2,1,0:T(8,128)(2,1)S(1)}, bf16[2,8,256,256]{3,2,1,0:T(8,128)(2,1)S(1)}, u32[]{:S(2)}, u32[]{:S(2)}) %collective-permute-start.3) | collective-permute-done | bytes 2097184 | tf_op jit(solution)/shard_map/ppermute | solution.py:26
  306.0 0.7 convolution_bitcast_fusion
  306.8 169.5 %collective-permute-done.2 = bf16[2,8,256,256]{3,2,1,0:T(8,128)(2,1)S(1)} collective-permute-done((bf16[2,8,256,256]{3,2,1,0:T(8,128)(2,1)S(1)}, bf16[2,8,256,256]{3,2,1,0:T(8,128)(2,1)S(1)}, u32[]{:S(2)}, u32[]{:S(2)}) %collective-permute-start.2) | collective-permute-done | bytes 2097184 | tf_op jit(solution)/shard_map/ppermute | solution.py:26
  476.3 0.7 convolution_bitcast_fusion.2
  477.1 0.7 convolution_bitcast_fusion.4
  477.8 0.7 convolution_bitcast_fusion.1
  478.6 0.7 convolution_bitcast_fusion.3
  479.4 0.7 convolution_bitcast_fusion.5
  480.2 1.5 maximum_bitcast_fusion
  (17 shorter events, 1.8 us)
Async XLA Ops:
  2.0 5.6 %copy-start = (bf16[256,4096]{1,0:T(8,128)(2,1)S(1)}, bf16[256,4096]{1,0:T(8,128)(2,1)}, u32[]{:S(2)}) copy-start(bf16[256,4096]{1,0:T(8,128)(2,1)} %param.1) | copy-start | bytes 6291460
  2.0 5.5 %collective-permute-start = (bf16[256,15,256]{2,0,1:T(8,128)(2,1)S(1)}, bf16[256,15,256]{2,0,1:T(8,128)(2,1)S(1)}, u32[]{:S(2)}, u32[]{:S(2)}) collective-permute-start(bf16[256,15,256]{2,0,1:T(8,128)(2,1)S(1)} %slice.165), channel_id=1, source_target_pairs={{0,1},{1,2},{2,3},{3,4},{4,5},{5,6},{6,7},{7,8},{8,9},{9,10},{10,1... | collective-permute-start | bytes 5898248 | tf_op jit(solution)/shard_map/ppermute | solution.py:20
  124.4 181.7 %collective-permute-start.3 = (bf16[2,8,256,256]{3,2,1,0:T(8,128)(2,1)S(1)}, bf16[2,8,256,256]{3,2,1,0:T(8,128)(2,1)S(1)}, u32[]{:S(2)}, u32[]{:S(2)}) collective-permute-start(bf16[2,8,256,256]{3,2,1,0:T(8,128)(2,1)S(1)} %fusion.1), channel_id=1, source_target_pairs={{0,48},{16,64},{32,80},{48,96},{64,112},{80,128},{96,144},{112,160... | collective-permute-start | bytes 6291464 | tf_op jit(solution)/shard_map/ppermute | solution.py:26
  129.1 347.2 %collective-permute-start.2 = (bf16[2,8,256,256]{3,2,1,0:T(8,128)(2,1)S(1)}, bf16[2,8,256,256]{3,2,1,0:T(8,128)(2,1)S(1)}, u32[]{:S(2)}, u32[]{:S(2)}) collective-permute-start(bf16[2,8,256,256]{3,2,1,0:T(8,128)(2,1)S(1)} %fusion.1), channel_id=1, source_target_pairs={{0,32},{16,48},{32,64},{48,80},{64,96},{80,112},{96,128},{112,144}... | collective-permute-start | bytes 6291464 | tf_op jit(solution)/shard_map/ppermute | solution.py:26
  241.0 236.1 %collective-permute-start.1 = (bf16[2,8,256,256]{3,2,1,0:T(8,128)(2,1)S(1)}, bf16[2,8,256,256]{3,2,1,0:T(8,128)(2,1)S(1)}, u32[]{:S(2)}, u32[]{:S(2)}) collective-permute-start(bf16[2,8,256,256]{3,2,1,0:T(8,128)(2,1)S(1)} %fusion.1), channel_id=1, source_target_pairs={{0,16},{16,32},{32,48},{48,64},{64,80},{80,96},{96,112},{112,128},... | collective-permute-start | bytes 6291464 | tf_op jit(solution)/shard_map/ppermute | solution.py:26
where the time goes:
time: 482 us
  waiting for transfers between devices  188 us (39%)
  starting transfers between devices  166 us (34%)
  blocking collectives  105 us (22%)
  matrix products  13.9 us (3%)
    ppermute x3, waiting for transfers between devices, from_behind(): return lax.ppermute(value, axis, pairs)  185 us
    ppermute x3, starting transfers between devices, from_behind(): return lax.ppermute(value, axis, pairs)  164 us
    all_to_all x1, blocking collectives, on_device(): lax.all_to_all(spectra, 'tm', split_axis=1, concat_axis=2, tiled=True)  105 us
  transfers between devices with their start and end apart: 4, of which 3 were waited for; matrix products, arithmetic and copies ran while one was open for 1% of the time, Pallas kernels for 0%

commit v1 on v0

v1 whole, which is shorter than its diff:
```python
import math

import jax
import jax.numpy as jnp
import numpy as np
from jax import lax
from jax.experimental import pallas as pl
from jax.experimental.pallas import tpu as pltpu
from jax.sharding import PartitionSpec as P

NFFT = 256
TAPS = 16
BINS = 128
CHANNELS = 256
GROUP = 8
LOCAL = 16
CHUNKS = 8
PER = LOCAL // CHUNKS
SLOTS = 16
EARLY = 7
ROW = 4

epsilon = 1e-06
MESH = pl.DeviceIdType.MESH


def prototype():
    centred = (np.arange(TAPS * NFFT, dtype=np.float64) + 0.5 - 0.5 * TAPS * NFFT) / NFFT
    window = np.sinc(centred) * (0.5 + 0.5 * np.cos(2.0 * math.pi * centred / TAPS))
    table = window.reshape(TAPS, 1, NFFT).astype(np.float32)
    return np.broadcast_to(table, (TAPS, 8, NFFT)).copy()


def transform_table():
    frequency = np.arange(BINS)[:, None]
    phases = (frequency * np.arange(NFFT)[None, :] % NFFT) * (2.0 * math.pi / NFFT)
    parts = np.stack([np.cos(phases), -np.sin(phases)]).reshape(2, 16, 8, NFFT)
    return jnp.asarray(parts.transpose(1, 0, 2, 3).reshape(2 * BINS, NFFT), jnp.bfloat16)


def kernel(samples, proto, fourier, out, frames, outgoing, incoming, both, crossing, spill, others,
           power, white, turned, y_send, y_recv, self_sem, z_send, z_recv, spill_send, spill_recv,
           up_send, up_recv, x_send, x_recv):
    chan, tm = lax.axis_index("chan"), lax.axis_index("tm")
    half, member = tm // GROUP, tm % GROUP
    place = chan % ROW
    n_chan, n_tm = lax.axis_size("chan"), lax.axis_size("tm")

    def peer(o):
        return (chan, half * GROUP + lax.rem(member + o, GROUP))

    def beside(o):
        return (chan - place + lax.rem(place + o, ROW), tm)

    opposite = (chan, lax.rem(tm + GROUP, n_tm))
    above = (lax.rem(chan + ROW, n_chan), tm)
    below = (lax.rem(chan + n_chan - ROW, n_chan), tm)

    barrier = pltpu.get_barrier_semaphore()
    greeted = [peer(o) for o in range(1, GROUP)] + [beside(o) for o in range(1, ROW)]
    greeted += [opposite, above, below]
    for device in greeted:
        pl.semaphore_signal(barrier, inc=1, device_id=device, device_id_type=MESH)
    pl.semaphore_wait(barrier, len(greeted))

    def remote(src, dst, send, recv, device):
        return pltpu.make_async_remote_copy(
            src_ref=src, dst_ref=dst, send_sem=send, recv_sem=recv,
            device_id=device, device_id_type=MESH)

    def y_copy(j, o):
        to = lax.rem(member + o, GROUP)
        return remote(outgoing.at[j, to], incoming.at[j, member], y_send.at[j, o - 1],
                      y_recv.at[j, o - 1], peer(o))

    def self_copy(j):
        return pltpu.make_async_copy(outgoing.at[j, member], incoming.at[j, member], self_sem.at[j])

    def z_copy(j):
        return remote(crossing.at[j], both.at[0, j, pl.ds(GROUP, GROUP)], z_send.at[j], z_recv.at[j],
                      opposite)

    def spill_copy(j):
        return remote(incoming.at[j, GROUP - 1, 1, 1], spill.at[j], spill_send.at[j],
                      spill_recv.at[j], opposite)

    spans = (pl.ds(0, EARLY), pl.ds(EARLY, SLOTS - EARLY))

    def up_copy(j, part):
        return remote(both.at[0, j, spans[part]], both.at[1, j, spans[part]], up_send.at[j, part],
                      up_recv.at[j, part], above)

    def x_copy(j, part, o, item):
        return remote(both.at[item, j, spans[part]], others.at[o - 1, j, spans[part]],
                      x_send.at[j, part, o - 1], x_recv.at[j, part, o - 1], beside(o))

    def send_own(j, part):
        up_copy(j, part).start()
        for o in range(1, ROW):
            @pl.when(place + o < ROW)
            def _():
                x_copy(j, part, o, 0).start()

    def send_below(j, part):
        up_copy(j, part).wait_recv()
        for o in range(1, ROW):
            @pl.when(place + o >= ROW)
            def _():
                x_copy(j, part, o, 1).start()

    per_group = 4
    for group in range(LOCAL // per_group):
        first = group * per_group

        @pl.loop(0, CHANNELS // 16)
        def _(tile):
            rows = pl.ds(pl.multiple_of(tile * 16, 16), 16)
            for side in range(2):
                lanes = pl.ds(side * 128, 128)
                blocks = [
                    samples[rows, pl.ds(m * NFFT + side * 128, 128)].astype(jnp.float32)
                    for m in range(LOCAL)
                ]
                taps = [proto[k, :, lanes] for k in range(TAPS)]
                for i in range(per_group):
                    s = first + i
                    for part, members in ((0, range(s + 1)), (1, range(s + 1, LOCAL))):
                        pieces = []
                        for h in range(2):
                            total = None
                            for m in members:
                                k = TAPS - 1 - s + m if part == 0 else m - s - 1
                                term = taps[k] * blocks[m][h * 8:(h + 1) * 8]
                                total = term if total is None else total + term
                            if total is None:
                                total = jnp.zeros((8, 128), jnp.float32)
                            pieces.append(total)
                        frames[i, part, rows, lanes] = jnp.concatenate(pieces, 0).astype(jnp.bfloat16)

        @pl.loop(0, per_group)
        def _(i):
            for part in range(2):
                result = lax.dot_general(
                    fourier[...], frames[i, part], (((1,), (1,)), ((), ())),
                    preferred_element_type=jnp.float32)
                result = result.astype(jnp.bfloat16).reshape(2, GROUP, 16, CHANNELS)
                j = (first + i) // PER
                for h in range(2):
                    outgoing[j, :, h, part, i % PER] = result[h]

        for j in range(first // PER, (first + per_group) // PER):
            self_copy(j).start()
            for o in range(1, GROUP):
                y_copy(j, o).start()

    def gather(j):
        self_copy(j).wait()
        for o in range(1, GROUP):
            y_copy(j, o).wait_recv()

        def total(k, which):
            value = incoming[j, k, which, 0].astype(jnp.float32)
            if k > 0:
                value = value + incoming[j, k - 1, which, 1].astype(jnp.float32)
            return value.astype(jnp.bfloat16)

        for k in range(GROUP):
            crossing[j, k] = total(k, 1 - half)
        z_copy(j).start()

        @pl.when(half == 0)
        def _():
            spill_copy(j).start()

        for k in range(GROUP):
            both[0, j, k - 1 if k > 0 else EARLY] = total(k, half)
        send_own(j, 0)

    def join(j):
        z_copy(j).wait_recv()

        @pl.when(half == 0)
        def _():
            both[0, j, GROUP] = (both[0, j, GROUP].astype(jnp.float32)
                                 + incoming[j, GROUP - 1, 0, 1].astype(jnp.float32)
                                 ).astype(jnp.bfloat16)

        @pl.when(half == 1)
        def _():
            spill_copy(j).wait_recv()
            both[0, j, EARLY] = (both[0, j, EARLY].astype(jnp.float32)
                                 + spill[j].astype(jnp.float32)).astype(jnp.bfloat16)

        send_own(j, 1)

    def add_power(which, read):
        total = power[which]
        for k in range(SLOTS):
            for i in range(PER):
                value = read(k, i).astype(jnp.float32)
                total = total + value * value
        power[which] = total

    power[...] = jnp.zeros_like(power)

    @pl.loop(0, CHUNKS)
    def _(j):
        gather(j)

    @pl.loop(0, CHUNKS)
    def _(j):
        join(j)
        send_below(j, 0)
        send_below(j, 1)
        add_power(0, lambda k, i: both[0, j, k, i])
        for o in range(1, ROW):
            for part in range(2):
                x_copy(j, part, o, 0).wait_recv()
            add_power(o, lambda k, i: others[o - 1, j, k, i])

    def scale(which):
        total = power[which]
        mean = (total[:8] + total[8:]) * (1.0 / (2 * GROUP * LOCAL))
        factor = lax.rsqrt(mean + epsilon)
        return jnp.concatenate([factor, factor], 0)

    span = SLOTS * PER * 16

    own = scale(0)

    @pl.loop(0, CHUNKS)
    def _(j):
        value = both[0, j].astype(jnp.float32).reshape(SLOTS * PER, 16, CHANNELS) * own[None]
        flipped = jnp.concatenate([value[:, 8:], -value[:, :8]], 1)
        value = value.reshape(span, CHANNELS).astype(jnp.bfloat16)
        white[j] = value
        columns = pl.ds(pl.multiple_of(j * span, span), span)
        turned[0, :, columns] = value.T
        turned[1, :, columns] = flipped.reshape(span, CHANNELS).astype(jnp.bfloat16).T

    def correlate(distance):
        partner = white[...].reshape(CHUNKS * span, CHANNELS)
        for i in range(2):
            out[distance, i] = jnp.dot(
                turned[i], partner, preferred_element_type=jnp.float32) * (1.0 / (2 * GROUP * LOCAL))

    correlate(0)
    for o in range(1, ROW):
        factor = scale(o)

        @pl.loop(0, CHUNKS)
        def _(j):
            value = others[o - 1, j].astype(jnp.float32).reshape(SLOTS * PER, 16, CHANNELS)
            white[j] = (value * factor[None]).reshape(span, CHANNELS).astype(jnp.bfloat16)

        correlate(o)

    @pl.loop(0, CHUNKS)
    def _(j):
        for o in range(1, GROUP):
            y_copy(j, o).wait_send()
        z_copy(j).wait_send()

        @pl.when(half == 0)
        def _():
            spill_copy(j).wait_send()

        for part in range(2):
            up_copy(j, part).wait_send()
            for o in range(1, ROW):
                x_copy(j, part, o, 0).wait_send()


def on_device(samples):
    chunk = (SLOTS, PER, 16, CHANNELS)
    rows = CHUNKS * SLOTS * PER * 16
    dma = pltpu.SemaphoreType.DMA
    vmem = pl.BlockSpec(memory_space=pltpu.VMEM)
    bf16 = jnp.bfloat16
    result = pl.pallas_call(
        kernel,
        out_shape=jax.ShapeDtypeStruct((ROW, 2, CHANNELS, CHANNELS), jnp.float32),
        in_specs=[vmem] * 3,
        out_specs=vmem,
        scratch_shapes=[
            pltpu.VMEM((4, 2, CHANNELS, NFFT), bf16),
            pltpu.VMEM((CHUNKS, GROUP, 2, 2, PER, 16, CHANNELS), bf16),
            pltpu.VMEM((CHUNKS, GROUP, 2, 2, PER, 16, CHANNELS), bf16),
            pltpu.VMEM((2, CHUNKS) + chunk, bf16),
            pltpu.VMEM((CHUNKS, GROUP, PER, 16, CHANNELS), bf16),
            pltpu.VMEM((CHUNKS, PER, 16, CHANNELS), bf16),
            pltpu.VMEM((ROW - 1, CHUNKS) + chunk, bf16),
            pltpu.VMEM((ROW, 16, CHANNELS), jnp.float32),
            pltpu.VMEM((CHUNKS, rows // CHUNKS, CHANNELS), bf16),
            pltpu.VMEM((2, CHANNELS, rows), bf16),
            dma((CHUNKS, GROUP - 1)), dma((CHUNKS, GROUP - 1)), dma((CHUNKS,)),
            dma((CHUNKS,)), dma((CHUNKS,)), dma((CHUNKS,)), dma((CHUNKS,)),
            dma((CHUNKS, 2)), dma((CHUNKS, 2)),
            dma((CHUNKS, 2, ROW - 1)), dma((CHUNKS, 2, ROW - 1)),
        ],
        compiler_params=pltpu.CompilerParams(
            collective_id=0, has_side_effects=True, vmem_limit_bytes=50 * 2**20),
        cost_estimate=pl.CostEstimate(flops=5 * 10**9, bytes_accessed=4 * 2**20, transcendentals=0),
    )(samples, prototype(), transform_table())
    return result[None]


def solution(mesh):
    return jax.shard_map(
        on_device,
        mesh=mesh,
        in_specs=(P("chan", "tm"),),
        out_specs=P("tm", None, None, "chan", None),
        check_vma=False,
    )
```

time: 482 us -> 261 us (0.54)
  the two profiles are of different devices: /device:TPU:64 before, /device:TPU:1 now
where the time goes in v1:
time: 261 us
  Pallas kernels  258 us (99%)
  local copies, waits for them, and re-layouts  3.13 us (1%)
    pallas_call x1, Pallas kernels, on_device(): pl.pallas_call(kernel, out_shape=jax.ShapeDtypeStruct((ROW, 2, CHANNELS,...  258 us

profile of v1, /device:TPU:1, one launch (start us, length us, event | category | flops | bytes accessed | tf_op | source)
XLA Modules:
  0.0 260.9 jit_solution(15002739598502126474)
XLA Ops:
  0.0 0.0 copy-start
  0.0 0.9 copy-done
  0.9 0.0 copy-start.1
  0.9 0.9 copy-done.1
  1.8 257.7 %shard_map.37 = f32[4,2,256,256]{3,2,1,0:T(8,128)S(1)} custom-call(bf16[256,4096]{1,0:T(8,128)(2,1)} %samples.1, f32[16,8,256]{2,1,0:T(8,128)S(1)} %copy-done, bf16[256,256]{1,0:T(8,128)(2,1)S(1)} %copy-done.1), custom_call_target="tpu_custom_call" | custom-call | flops 5000000000 | bytes 4194304 | tf_op jit(solution)/shard_map/pallas_call | solution.py:280
  259.5 1.3 copy.5
Async XLA Ops:
  0.0 0.9 copy-start
  0.9 0.9 copy-start.1

commit v2 on v1

--- a/solution.py
+++ b/solution.py
@@ -17,7 +17,10 @@
 CHUNKS = 8
 PER = LOCAL // CHUNKS
 SLOTS = 16
-EARLY = 7
+SPANS = ((0, 7), (7, 5), (12, 4))
+AHEAD_Y = 2
+AHEAD_Z = 1
+STEPS = (2, 2, 4, 4, 4)
 ROW = 4
 
 epsilon = 1e-06
@@ -38,9 +41,10 @@
     return jnp.asarray(parts.transpose(1, 0, 2, 3).reshape(2 * BINS, NFFT), jnp.bfloat16)
 
 
-def kernel(samples, proto, fourier, out, frames, outgoing, incoming, both, crossing, spill, others,
-           power, white, turned, y_send, y_recv, self_sem, z_send, z_recv, spill_send, spill_recv,
-           up_send, up_recv, x_send, x_recv):
+def kernel(samples_hbm, proto_hbm, fourier_hbm, out, samples, proto, fourier, frames, outgoing,
+           incoming, both, crossing, passing, spill, others, power, white, turned, in_sem, y_send,
+           y_recv, self_sem, z_send, z_recv, hop_send, hop_recv, spill_send, spill_recv, up_send,
+           up_recv, x_send, x_recv):
     chan, tm = lax.axis_index("chan"), lax.axis_index("tm")
     half, member = tm // GROUP, tm % GROUP
     place = chan % ROW
@@ -56,12 +60,24 @@
     above = (lax.rem(chan + ROW, n_chan), tm)
     below = (lax.rem(chan + n_chan - ROW, n_chan), tm)
 
+    far_above = (above[0], opposite[1])
+    far_below = (below[0], opposite[1])
+
+    inputs = [
+        pltpu.make_async_copy(src, dst, in_sem.at[i])
+        for i, (src, dst) in enumerate(
+            ((samples_hbm, samples), (proto_hbm, proto), (fourier_hbm, fourier)))
+    ]
+    for copy in inputs:
+        copy.start()
     barrier = pltpu.get_barrier_semaphore()
     greeted = [peer(o) for o in range(1, GROUP)] + [beside(o) for o in range(1, ROW)]
-    greeted += [opposite, above, below]
+    greeted += [opposite, above, below, far_above, far_below]
     for device in greeted:
         pl.semaphore_signal(barrier, inc=1, device_id=device, device_id_type=MESH)
     pl.semaphore_wait(barrier, len(greeted))
+    for copy in inputs:
+        copy.wait()
 
     def remote(src, dst, send, recv, device):
         return pltpu.make_async_remote_copy(
@@ -76,15 +92,26 @@
     def self_copy(j):
         return pltpu.make_async_copy(outgoing.at[j, member], incoming.at[j, member], self_sem.at[j])
 
-    def z_copy(j):
-        return remote(crossing.at[j], both.at[0, j, pl.ds(GROUP, GROUP)], z_send.at[j], z_recv.at[j],
-                      opposite)
+    upper, lower = pl.ds(GROUP + 4, 4), pl.ds(GROUP, 4)
+
+    def z_copy(j, way):
+        if way == 0:
+            return remote(crossing.at[j, pl.ds(4, 4)], both.at[1, j, upper], z_send.at[j, 0],
+                          z_recv.at[j, 0], far_above)
+        return remote(crossing.at[j, pl.ds(0, 4)], passing.at[j], z_send.at[j, 1], z_recv.at[j, 1],
+                      far_below)
+
+    def hop_copy(j, way):
+        if way == 0:
+            return remote(both.at[1, j, upper], both.at[0, j, upper], hop_send.at[j, 0],
+                          hop_recv.at[j, 0], below)
+        return remote(passing.at[j], both.at[0, j, lower], hop_send.at[j, 1], hop_recv.at[j, 1], above)
 
     def spill_copy(j):
         return remote(incoming.at[j, GROUP - 1, 1, 1], spill.at[j], spill_send.at[j],
                       spill_recv.at[j], opposite)
 
-    spans = (pl.ds(0, EARLY), pl.ds(EARLY, SLOTS - EARLY))
+    spans = tuple(pl.ds(*span) for span in SPANS)
 
     def up_copy(j, part):
         return remote(both.at[0, j, spans[part]], both.at[1, j, spans[part]], up_send.at[j, part],
@@ -95,22 +122,28 @@
                       x_send.at[j, part, o - 1], x_recv.at[j, part, o - 1], beside(o))
 
     def send_own(j, part):
-        up_copy(j, part).start()
+        if part < 2:
+            up_copy(j, part).start()
         for o in range(1, ROW):
             @pl.when(place + o < ROW)
             def _():
                 x_copy(j, part, o, 0).start()
 
     def send_below(j, part):
-        up_copy(j, part).wait_recv()
+        if part < 2:
+            up_copy(j, part).wait_recv()
         for o in range(1, ROW):
             @pl.when(place + o >= ROW)
             def _():
                 x_copy(j, part, o, 1).start()
 
-    per_group = 4
-    for group in range(LOCAL // per_group):
-        first = group * per_group
+    def relay(j, way):
+        z_copy(j, way).wait_recv()
+        hop_copy(j, way).start()
+        if way == 0:
+            send_below(j, 2)
+
+    def transform(first, per_group):
 
         @pl.loop(0, CHANNELS // 16)
         def _(tile):
@@ -148,10 +181,10 @@
                 for h in range(2):
                     outgoing[j, :, h, part, i % PER] = result[h]
 
-        for j in range(first // PER, (first + per_group) // PER):
-            self_copy(j).start()
-            for o in range(1, GROUP):
-                y_copy(j, o).start()
+    def spread(j):
+        self_copy(j).start()
+        for o in range(1, GROUP):
+            y_copy(j, o).start()
 
     def gather(j):
         self_copy(j).wait()
@@ -166,18 +199,19 @@
 
         for k in range(GROUP):
             crossing[j, k] = total(k, 1 - half)
-        z_copy(j).start()
+        for way in range(2):
+            z_copy(j, way).start()
 
         @pl.when(half == 0)
         def _():
             spill_copy(j).start()
 
         for k in range(GROUP):
-            both[0, j, k - 1 if k > 0 else EARLY] = total(k, half)
+            both[0, j, k - 1 if k > 0 else GROUP - 1] = total(k, half)
         send_own(j, 0)
 
     def join(j):
-        z_copy(j).wait_recv()
+        hop_copy(j, 1).wait_recv()
 
         @pl.when(half == 0)
         def _():
@@ -188,10 +222,13 @@
         @pl.when(half == 1)
         def _():
             spill_copy(j).wait_recv()
-            both[0, j, EARLY] = (both[0, j, EARLY].astype(jnp.float32)
+            both[0, j, GROUP - 1] = (both[0, j, GROUP - 1].astype(jnp.float32)
                                  + spill[j].astype(jnp.float32)).astype(jnp.bfloat16)
 
         send_own(j, 1)
+        hop_copy(j, 0).wait_recv()
+        send_own(j, 2)
+        add_power(0, lambda k, i: both[0, j, k, i])
 
     def add_power(which, read):
         total = power[which]
@@ -203,20 +240,51 @@
 
     power[...] = jnp.zeros_like(power)
 
-    @pl.loop(0, CHUNKS)
-    def _(j):
-        gather(j)
-
-    @pl.loop(0, CHUNKS)
-    def _(j):
-        join(j)
-        send_below(j, 0)
-        send_below(j, 1)
-        add_power(0, lambda k, i: both[0, j, k, i])
+    def collect(j):
         for o in range(1, ROW):
-            for part in range(2):
+            for part in range(len(SPANS)):
                 x_copy(j, part, o, 0).wait_recv()
             add_power(o, lambda k, i: others[o - 1, j, k, i])
+
+    first = spread_up_to = 0
+    for count, step in enumerate(STEPS):
+        if count == 2:
+            gather(0)
+        transform(first, step)
+        first += step
+        while spread_up_to < AHEAD_Y and (spread_up_to + 1) * PER <= first:
+            spread(spread_up_to)
+            spread_up_to += 1
+    for j in range(1, AHEAD_Z):
+        gather(j)
+
+    @pl.loop(0, CHUNKS + 2)
+    def _(j):
+        @pl.when(j + AHEAD_Y < CHUNKS)
+        def _():
+            spread(j + AHEAD_Y)
+
+        @pl.when(j + AHEAD_Z < CHUNKS)
+        def _():
+            gather(j + AHEAD_Z)
+
+        @pl.when((j >= 1) & (j <= CHUNKS))
+        def _():
+            join(j - 1)
+
+        @pl.when(j >= 2)
+        def _():
+            send_below(j - 2, 1)
+
+        @pl.when(j < CHUNKS)
+        def _():
+            send_below(j, 0)
+            for way in range(2):
+                relay(j, way)
+
+        @pl.when(j >= 3)
+        def _():
+            collect(j - 3)
 
     def scale(which):
         total = power[which]
@@ -245,6 +313,7 @@
                 turned[i], partner, preferred_element_type=jnp.float32) * (1.0 / (2 * GROUP * LOCAL))
 
     correlate(0)
+    collect(CHUNKS - 1)
     for o in range(1, ROW):
         factor = scale(o)
 
@@ -259,14 +328,17 @@
     def _(j):
         for o in range(1, GROUP):
             y_copy(j, o).wait_send()
-        z_copy(j).wait_send()
+        for way in range(2):
+            z_copy(j, way).wait_send()
+            hop_copy(j, way).wait_send()
 
         @pl.when(half == 0)
         def _():
             spill_copy(j).wait_send()
 
-        for part in range(2):
-            up_copy(j, part).wait_send()
+        for part in range(len(SPANS)):
+            if part < 2:
+                up_copy(j, part).wait_send()
             for o in range(1, ROW):
                 x_copy(j, part, o, 0).wait_send()
 
@@ -280,23 +352,27 @@
     result = pl.pallas_call(
         kernel,
         out_shape=jax.ShapeDtypeStruct((ROW, 2, CHANNELS, CHANNELS), jnp.float32),
-        in_specs=[vmem] * 3,
+        in_specs=[pl.BlockSpec(memory_space=pl.ANY)] * 3,
         out_specs=vmem,
         scratch_shapes=[
-            pltpu.VMEM((4, 2, CHANNELS, NFFT), bf16),
+            pltpu.VMEM(samples.shape, bf16),
+            pltpu.VMEM((TAPS, 8, NFFT), jnp.float32),
+            pltpu.VMEM((2 * BINS, NFFT), bf16),
+            pltpu.VMEM((max(STEPS), 2, CHANNELS, NFFT), bf16),
             pltpu.VMEM((CHUNKS, GROUP, 2, 2, PER, 16, CHANNELS), bf16),
             pltpu.VMEM((CHUNKS, GROUP, 2, 2, PER, 16, CHANNELS), bf16),
             pltpu.VMEM((2, CHUNKS) + chunk, bf16),
             pltpu.VMEM((CHUNKS, GROUP, PER, 16, CHANNELS), bf16),
+            pltpu.VMEM((CHUNKS, GROUP // 2, PER, 16, CHANNELS), bf16),
             pltpu.VMEM((CHUNKS, PER, 16, CHANNELS), bf16),
             pltpu.VMEM((ROW - 1, CHUNKS) + chunk, bf16),
             pltpu.VMEM((ROW, 16, CHANNELS), jnp.float32),
             pltpu.VMEM((CHUNKS, rows // CHUNKS, CHANNELS), bf16),
             pltpu.VMEM((2, CHANNELS, rows), bf16),
-            dma((CHUNKS, GROUP - 1)), dma((CHUNKS, GROUP - 1)), dma((CHUNKS,)),
-            dma((CHUNKS,)), dma((CHUNKS,)), dma((CHUNKS,)), dma((CHUNKS,)),
-            dma((CHUNKS, 2)), dma((CHUNKS, 2)),
-            dma((CHUNKS, 2, ROW - 1)), dma((CHUNKS, 2, ROW - 1)),
+            dma((3,)), dma((CHUNKS, GROUP - 1)), dma((CHUNKS, GROUP - 1)), dma((CHUNKS,)),
+            dma((CHUNKS, 2)), dma((CHUNKS, 2)), dma((CHUNKS, 2)), dma((CHUNKS, 2)),
+            dma((CHUNKS,)), dma((CHUNKS,)), dma((CHUNKS, 2)), dma((CHUNKS, 2)),
+            dma((CHUNKS, len(SPANS), ROW - 1)), dma((CHUNKS, len(SPANS), ROW - 1)),
         ],
         compiler_params=pltpu.CompilerParams(
             collective_id=0, has_side_effects=True, vmem_limit_bytes=50 * 2**20),

time: 261 us -> 197 us (0.75)
  Pallas kernels: 258 us -> 193 us
    pallas_call x1, Pallas kernels: 258 us -> 193 us  [on_device(): pl.pallas_call(kernel, out_shape=jax.ShapeDtypeStruct((ROW, 2, CHANNELS,...]
where the time goes in v2:
time: 197 us; the launch traced here: 196 us
  Pallas kernels  193 us (98%)
  local copies, waits for them, and re-layouts  3.13 us (2%)
    pallas_call x1, Pallas kernels, on_device(): pl.pallas_call(kernel, out_shape=jax.ShapeDtypeStruct((ROW, 2, CHANNELS,...  193 us

profile of v2, /device:TPU:1, one launch (start us, length us, event | category | flops | bytes accessed | tf_op | source)
XLA Modules:
  0.0 196.2 jit_solution(8186307378667421720)
XLA Ops:
  0.0 0.0 copy-start
  0.0 0.9 copy-done
  0.9 0.0 copy-start.1
  0.9 0.9 copy-done.1
  1.8 193.1 %shard_map.37 = f32[4,2,256,256]{3,2,1,0:T(8,128)S(1)} custom-call(bf16[256,4096]{1,0:T(8,128)(2,1)} %samples_hbm.1, f32[16,8,256]{2,1,0:T(8,128)S(1)} %copy-done, bf16[256,256]{1,0:T(8,128)(2,1)S(1)} %copy-done.1), custom_call_target="tpu_custom_call" | custom-call | flops 5000000000 | bytes 4194304 | tf_op jit(solution)/shard_map/pallas_call | solution.py:352
  194.9 1.3 copy.5
Async XLA Ops:
  0.0 0.9 copy-start
  0.9 0.9 copy-start.1

commit v3 on v2

--- a/solution.py
+++ b/solution.py
@@ -268,19 +268,19 @@
         def _():
             gather(j + AHEAD_Z)
 
-        @pl.when((j >= 1) & (j <= CHUNKS))
-        def _():
-            join(j - 1)
-
-        @pl.when(j >= 2)
-        def _():
-            send_below(j - 2, 1)
-
         @pl.when(j < CHUNKS)
         def _():
             send_below(j, 0)
             for way in range(2):
                 relay(j, way)
+
+        @pl.when((j >= 1) & (j <= CHUNKS))
+        def _():
+            join(j - 1)
+
+        @pl.when(j >= 2)
+        def _():
+            send_below(j - 2, 1)
 
         @pl.when(j >= 3)
         def _():

time: 197 us -> 188 us (0.954)
  Pallas kernels: 193 us -> 184 us
    pallas_call x1, Pallas kernels: 193 us -> 184 us  [on_device(): pl.pallas_call(kernel, out_shape=jax.ShapeDtypeStruct((ROW, 2, CHANNELS,...]
where the time goes in v3:
time: 188 us; the launch traced here: 187 us
  Pallas kernels  184 us (98%)
  local copies, waits for them, and re-layouts  3.13 us (2%)
    pallas_call x1, Pallas kernels, on_device(): pl.pallas_call(kernel, out_shape=jax.ShapeDtypeStruct((ROW, 2, CHANNELS,...  184 us

profile of v3, /device:TPU:1, one launch (start us, length us, event | category | flops | bytes accessed | tf_op | source)
XLA Modules:
  0.0 187.1 jit_solution(2140700735848077426)
XLA Ops:
  0.0 0.0 copy-start
  0.0 0.9 copy-done
  0.9 0.0 copy-start.1
  0.9 0.9 copy-done.1
  1.8 184.0 %shard_map.37 = f32[4,2,256,256]{3,2,1,0:T(8,128)S(1)} custom-call(bf16[256,4096]{1,0:T(8,128)(2,1)} %samples_hbm.1, f32[16,8,256]{2,1,0:T(8,128)S(1)} %copy-done, bf16[256,256]{1,0:T(8,128)(2,1)S(1)} %copy-done.1), custom_call_target="tpu_custom_call" | custom-call | flops 5000000000 | bytes 4194304 | tf_op jit(solution)/shard_map/pallas_call | solution.py:352
  185.8 1.3 copy.5
Async XLA Ops:
  0.0 0.9 copy-start
  0.9 0.9 copy-start.1
